TPU v7x, 256 devices: a whole 4x4x8 slice. The times are simulated.
256 devices in a mesh: dp: 32 (over y, z_hi, core), seq: 8 (over x, z_lo).
Axes of the slice: x: 4, y: 4, z: 8 (z_hi: 4, z_lo: 2; z = z_hi * 2 + z_lo), core: 2. Of those that a mesh axis runs over, the one named last changes fastest.
Arguments:
- tokens: bfloat16 [32, 8192, 768], P('dp', 'seq'), may hold values from -6 to 6
- depthwise_weight: float32 [3, 768], replicated, may hold values from -4 to 4
- down_weight: bfloat16 [1536, 1536], replicated, may hold values from -0.15625 to 0.15625
- bott_dw: float32 [3, 1536], replicated, may hold values from -4 to 4
- bott_weight: bfloat16 [1536, 768], replicated, may hold values from -0.15625 to 0.15625
- cotangent: bfloat16 [32, 4096, 768], P('dp', 'seq'), may hold values from -6 to 6
- plan_owner: int32 [32, 256], P('dp'), may hold values from 0 to 7, as said below
- plan_slot: int32 [32, 256], P('dp'), may hold values from 0 to 3, as said below
- counts: int32 [32, 8], P('dp'), may hold values from 8 to 32, as said below
Outputs:
- owned_panels: bfloat16 [32, 256, 16, 1536], P('dp', 'seq')
- bottleneck: bfloat16 [32, 4096, 768], P('dp', 'seq')
- grad_bott: float32 [1536, 768], P(('dp', 'seq'))
Inputs may be any that keep to these rules, and one draw needn't show every extreme that they name: `plan_owner`: for each window and each source device s, the 32 groups of s fill each owner's 4 slots 0 to 3 for s exactly once: no two groups of s share an owner and slot. `plan_slot`: slot of a group among the groups its source sends to its owner. `counts`: in every window some device has all 32 groups mappable.
All inputs are finite; a program needn't handle non-finite values.
Results may differ from a plain program's by a relative error of at most 0.013.
Values may be sent and summed in bfloat16 or wider, within the bound.
A program may use at most 128 MiB of HBM per device.

v0:
```python
import jax
import jax.numpy as jnp
from jax import lax
from jax.sharding import PartitionSpec as P

C = 768
C2 = 1536
GROUP = 32
DILATION_STEP = 8
GROUPS_DEV = 32
HALF = 16


def padded(block, sides, width):
    for axis, dim in sides:
        count = lax.axis_size(axis)
        forward = [(i, i + 1) for i in range(count - 1)]
        backward = [(target, source) for source, target in forward]
        low = lax.ppermute(
            lax.slice_in_dim(block, block.shape[dim] - width, None, axis=dim), axis, forward
        )
        high = lax.ppermute(lax.slice_in_dim(block, 0, width, axis=dim), axis, backward)
        block = jnp.concatenate([low, block, high], axis=dim)
    return block


def on_device(
    tokens,
    depthwise_weight,
    down_weight,
    bott_dw,
    bott_weight,
    cotangent,
    plan_owner,
    plan_slot,
    counts,
):
    n_seq = lax.axis_size("seq")
    me_seq = lax.axis_index("seq")
    per_pair = GROUPS_DEV // n_seq
    windows = tokens.shape[0]
    sequence_length = tokens.shape[1]
    padded_input = padded(tokens, (("seq", 1),), DILATION_STEP).astype(jnp.float32)
    conv_result = (
        depthwise_weight[0] * padded_input[:, 0:sequence_length]
        + depthwise_weight[1] * padded_input[:, DILATION_STEP : DILATION_STEP + sequence_length]
        + depthwise_weight[2]
        * padded_input[:, 2 * DILATION_STEP : 2 * DILATION_STEP + sequence_length]
    )
    act = (tokens.astype(jnp.float32) + jax.nn.gelu(conv_result)).astype(jnp.bfloat16)
    grouped = act.reshape(windows, GROUPS_DEV, GROUP, C)
    my_owner = lax.dynamic_slice_in_dim(plan_owner, me_seq * GROUPS_DEV, GROUPS_DEV, 1)
    my_slot = lax.dynamic_slice_in_dim(plan_slot, me_seq * GROUPS_DEV, GROUPS_DEV, 1)
    my_count = lax.dynamic_slice_in_dim(counts, me_seq, 1, 1)
    places = my_owner * per_pair + my_slot
    column = lax.iota(jnp.int32, GROUPS_DEV)
    live = column[None, :] < my_count
    placer = ((places[:, None, :] == column[None, :, None]) & live[:, None, :]).astype(jnp.bfloat16)
    outgoing = jnp.einsum(
        "wpj,wjrc->wprc", placer, grouped, preferred_element_type=jnp.float32
    ).astype(jnp.bfloat16)
    outgoing = outgoing.reshape(windows, n_seq, per_pair, GROUP, C)
    arrived = lax.all_to_all(outgoing, "seq", split_axis=1, concat_axis=1, tiled=True)
    shape_now = arrived.shape
    pairs = arrived.reshape(shape_now[0], shape_now[1], shape_now[2], HALF, 2 * C)
    projected = jnp.einsum(
        "wnkhd,de->wnkhe", pairs, down_weight, preferred_element_type=jnp.float32
    )
    panels = jax.nn.gelu(projected).astype(jnp.bfloat16)
    owned = panels.reshape(windows, GROUPS_DEV, HALF, C2)
    everything = lax.all_gather(owned, "seq", axis=1, tiled=True)
    total_groups = plan_owner.shape[1]
    source = lax.iota(jnp.int32, total_groups) // GROUPS_DEV
    where_all = plan_owner * GROUPS_DEV + source[None, :] * per_pair + plan_slot
    mine_index = lax.dynamic_slice_in_dim(where_all, me_seq * GROUPS_DEV, GROUPS_DEV, 1)
    mine = jnp.take_along_axis(everything, mine_index[:, :, None, None], axis=1)
    local_rows = mine.reshape(windows, GROUPS_DEV * HALF, C2)
    extended = padded(local_rows, (("seq", 1),), 1)
    extended = extended.astype(jnp.float32)
    rows = extended.shape[1] - 2
    mixed = (
        bott_dw[0] * extended[:, 0:rows]
        + bott_dw[1] * extended[:, 1 : rows + 1]
        + bott_dw[2] * extended[:, 2 : rows + 2]
    ).astype(jnp.bfloat16)
    pre = jnp.einsum("wtc,ce->wte", mixed, bott_weight, preferred_element_type=jnp.float32)
    result, pullback = jax.vjp(jax.nn.gelu, pre)
    delta = pullback(cotangent.astype(jnp.float32))[0].astype(jnp.bfloat16)
    flat_mixed = mixed.reshape(windows * rows, C2)
    flat_delta = delta.reshape(windows * rows, C)
    share = C2 // lax.axis_size(("dp", "seq"))
    term = lax.dot_general(
        flat_mixed, flat_delta, (((0,), (0,)), ((), ())), preferred_element_type=jnp.float32
    )
    summed = lax.psum(term, ("dp", "seq"))
    grad_rows = lax.dynamic_slice_in_dim(summed, lax.axis_index(("dp", "seq")) * share, share, 0)
    return (owned, result.astype(jnp.bfloat16), grad_rows)


def solution(mesh):
    placed = (
        P("dp", "seq", None),
        P(),
        P(),
        P(),
        P(),
        P("dp", "seq", None),
        P("dp", None),
        P("dp", None),
        P("dp", None),
    )
    return jax.shard_map(
        on_device,
        mesh=mesh,
        in_specs=placed,
        out_specs=(P("dp", "seq", None, None), P("dp", "seq", None), P(("dp", "seq"), None)),
        check_vma=False,
    )
```

profile of v0, /device:TPU:2, one launch (start us, length us, event | category | flops | bytes accessed | tf_op | source)
XLA Modules:
  0.0 625.5 jit_solution(2044142660677475417)
XLA Ops:
  7.2 0.0 copy-start
  7.2 0.0 all-gather.2.cloned.1.call-start
  7.2 0.9 fusion.65
  8.1 3.8 collective-permute-start.1
  11.9 2.0 collective-permute-start
  14.0 0.8 slice_reduce_fusion.5
  14.8 1.2 constant_dynamic-slice_fusion.3
  16.1 0.6 iota_compare_fusion.1
  16.7 0.8 add_bitcast_fusion
  17.5 0.0 copy-start.2
  17.5 0.0 collective-permute-done.1
  17.5 0.9 collective-permute-done
  18.4 1.6 maximum_convert_fusion
  20.0 0.0 copy-done.2
  20.0 1.9 fusion.10
  21.9 2.6 convolution_convert_fusion
  24.5 3.9 reshape.356
  28.4 1.9 copy.17
  30.3 25.1 %all_to_all.5 = bf16[1,8,4,32,768]{4,2,3,0,1:T(4,128)(2,1)S(1)} all-to-all(bf16[1,8,4,32,768]{4,2,3,0,1:T(4,128)(2,1)S(1)} %copy.17), channel_id=1, replica_groups=mesh['dp'=32,'seq'=8] {'seq'}, dimensions={1} | all-to-all | bytes 3145728 | tf_op jit(solution)/shard_map/all_to_all | solution.py:63
  55.5 1.4 copy.18
  56.9 3.6 reshape.357
  60.5 7.0 %fusion.25 = bf16[8,4,16,1536]{3,2,1,0:T(8,128)(2,1)} fusion(bf16[8,4,16,1536]{3,2,1,0:T(8,128)(2,1)} %reshape.357, bf16[1536,1536]{1,0:T(8,128)(2,1)} %param.11), kind=kOutput, calls=%fused_computation.32 | convolution fusion | flops 2422996992 | bytes 7864320 | tf_op jit(solution)/shard_map/wnkhd,de->wnkhe/dot_general | solution.py:66
  67.6 0.0 copy-start.5
  67.6 0.0 copy-start.6
  67.6 0.0 copy-start.4
  67.6 0.0 all-gather.2.cloned.1.call-update
  67.6 0.0 all-reduce.2.cloned.1.call-start
  67.6 0.6 copy-done.5
  68.2 0.0 copy-done.6
  68.2 0.1 compare_and_fusion
  68.3 0.1 broadcast_in_dim.27
  68.4 0.1 broadcast_in_dim.28
  68.5 0.0 copy-done.4
  68.5 0.1 slice_reduce_fusion.2
  68.6 250.2 %all-gather.2.cloned.1.call-done = bf16[1,256,16,1536]{3,2,0,1:T(8,128)(2,1)} async-done(((bf16[1,32,16,1536]{3,2,0,1:T(8,128)(2,1)}), bf16[1,256,16,1536]{3,2,0,1:T(8,128)(2,1)}) %all-gather.2.cloned.1.call-update) | async-done | bytes 12582928 | tf_op jit(solution)/shard_map/all_gather | solution.py:71
  318.8 6.4 %gather_fusion = bf16[32,16,1536]{2,1,0:T(8,128)(2,1)} fusion(bf16[256,16,1536]{2,1,0:T(8,128)(2,1)} %bitcast.80, s32[1024]{0:T(1024)S(1)} %pad_clamp_fusion), kind=kCustom, calls=%fused_computation | custom fusion | bytes 3145856 | tf_op jit(solution)/shard_map/jit(take_along_axis)/gather | solution.py:76
  325.2 0.0 copy-start.1
  325.2 1.7 bitcast_select_fusion.1
  326.9 3.3 collective-permute-start.3
  330.2 2.7 collective-permute-start.2
  333.0 0.0 copy-done.1
  333.0 0.3 bitcast_select_fusion
  333.3 0.0 collective-permute-done.3
  333.3 3.3 collective-permute-done.2
  336.7 0.5 maximum_convert_fusion.1
  337.1 1.0 fusion.39
  338.1 0.0 copy-done
  338.1 0.0 copy-start.7
  338.1 1.4 fusion.66
  339.5 0.0 copy-start.3
  339.5 1.2 copy-done.3
  340.7 0.0 copy-done.7
  340.7 4.0 fusion.41
  344.7 0.0 all-reduce.2.cloned.1.call-update
  344.7 2.8 fusion.51
  347.5 269.7 %all-reduce.2.cloned.1.call-done = f32[1536,768]{1,0:T(8,128)} async-done(((f32[1536,768]{1,0:T(8,128)}), f32[1536,768]{1,0:T(8,128)}) %all-reduce.2.cloned.1.call-update) | async-done | bytes 4718608 | tf_op jit(solution)/shard_map/psum | solution.py:95
  617.2 1.4 constant_dynamic-slice_fusion.1
  (4 shorter events, 0.0 us)
Async XLA Ops:
  7.2 331.0 %copy-start = (bf16[1536,768]{1,0:T(8,128)(2,1)S(1)}, bf16[1536,768]{1,0:T(8,128)(2,1)}, u32[]{:S(2)}) copy-start(bf16[1536,768]{1,0:T(8,128)(2,1)} %param.13) | copy-start | bytes 7077892
  7.2 311.6 %all-gather.2.cloned.1.call-start = ((), (), s32[]{:S(2)}) async-start(), calls=%async_computation.1 | async-start | bytes 14155776 | tf_op jit(solution)/shard_map/all_gather | solution.py:71
  8.1 9.4 %collective-permute-start.1 = (bf16[1,8,768]{2,1,0:T(8,128)(2,1)S(1)}, bf16[1,8,768]{2,1,0:T(8,128)(2,1)S(1)}, u32[]{:S(2)}, u32[]{:S(2)}) collective-permute-start(bf16[1,8,768]{2,1,0:T(8,128)(2,1)S(1)} %get-tuple-element.14), channel_id=1, source_target_pairs={{1,0},{2,1},{3,2},{4,3},{5,4},{6,5},{7,6},{9,8},{10,9},{11,10},{12... | collective-permute-start | bytes 36872 | tf_op jit(solution)/shard_map/ppermute | solution.py:22
  11.9 6.5 %collective-permute-start = (bf16[1,8,768]{2,1,0:T(8,128)(2,1)S(1)}, bf16[1,8,768]{2,1,0:T(8,128)(2,1)S(1)}, u32[]{:S(2)}, u32[]{:S(2)}) collective-permute-start(bf16[1,8,768]{2,1,0:T(8,128)(2,1)S(1)} %get-tuple-element.13), channel_id=1, source_target_pairs={{0,1},{1,2},{2,3},{3,4},{4,5},{5,6},{6,7},{8,9},{9,10},{10,11},{11... | collective-permute-start | bytes 36872 | tf_op jit(solution)/shard_map/ppermute | solution.py:19
  17.5 2.6 copy-start.2
  67.6 0.7 copy-start.5
  67.6 0.7 copy-start.6
  67.6 1.0 copy-start.4
  67.6 549.6 %all-reduce.2.cloned.1.call-start = ((), (), s32[]{:S(2)}) async-start(), calls=%async_computation.2 | async-start | bytes 9437184 | tf_op jit(solution)/shard_map/psum | solution.py:95
  325.2 7.8 %copy-start.1 = (bf16[32,16,1536]{2,1,0:T(8,128)(2,1)S(1)}, bf16[32,16,1536]{2,1,0:T(8,128)(2,1)}, u32[]{:S(2)}) copy-start(bf16[32,16,1536]{2,1,0:T(8,128)(2,1)} %gather_fusion) | copy-start | bytes 4718596
  326.9 6.4 %collective-permute-start.3 = (bf16[1,1,1536]{2,1,0:T(2,128)(2,1)S(1)}, bf16[1,1,1536]{2,1,0:T(2,128)(2,1)S(1)}, u32[]{:S(2)}, u32[]{:S(2)}) collective-permute-start(bf16[1,1,1536]{2,1,0:T(2,128)(2,1)S(1)} %get-tuple-element.12), channel_id=1, source_target_pairs={{1,0},{2,1},{3,2},{4,3},{5,4},{6,5},{7,6},{9,8},{10,9},{11,10},{12... | collective-permute-start | bytes 9224 | tf_op jit(solution)/shard_map/ppermute | solution.py:22
  330.2 6.4 %collective-permute-start.2 = (bf16[1,1,1536]{2,1,0:T(2,128)(2,1)S(1)}, bf16[1,1,1536]{2,1,0:T(2,128)(2,1)S(1)}, u32[]{:S(2)}, u32[]{:S(2)}) collective-permute-start(bf16[1,1,1536]{2,1,0:T(2,128)(2,1)S(1)} %get-tuple-element.11), channel_id=1, source_target_pairs={{0,1},{1,2},{2,3},{3,4},{4,5},{5,6},{6,7},{8,9},{9,10},{10,11},{11... | collective-permute-start | bytes 9224 | tf_op jit(solution)/shard_map/ppermute | solution.py:19
  338.1 2.6 copy-start.7
  339.5 1.2 copy-start.3
Sparse Core Ops, SparseCore 0:
  67.7 251.0 all-gather.1
  344.9 272.3 all-reduce.1
where the time goes:
time: 626 us; the launch traced here: 625 us
  waiting for transfers between devices  524 us (84%)
  blocking collectives  25.1 us (4%)
  local copies, waits for them, and re-layouts  23.7 us (4%)
  matrix products  15 us (2%)
  between operations  14.3 us (2%)
  starting transfers between devices  11.9 us (2%)
  other arithmetic  11.3 us (2%)
    psum x1, waiting for transfers between devices, on_device(): summed = lax.psum(term, ('dp', 'seq'))  270 us
    all_gather x1, waiting for transfers between devices, on_device(): everything = lax.all_gather(owned, 'seq', axis=1, tiled=True)  250 us
    all_to_all x1, blocking collectives, on_device(): lax.all_to_all(outgoing, 'seq', split_axis=1, concat_axis=1, tiled=True)  25.1 us
  transfers between devices with their start and end apart: 6, of which 4 were waited for; matrix products, arithmetic and copies ran while one was open for 1% of the time, Pallas kernels for 0%

commit v1 on v0

v1 whole, which is shorter than its diff:
```python
import jax
import jax.numpy as jnp
from jax import lax
from jax.experimental import pallas as pl
from jax.experimental.pallas import tpu as pltpu
from jax.sharding import PartitionSpec as P

C = 768
C2 = 1536
GROUP = 32
GROUPS_DEV = 32
HALF = 16
CAP = 4
N_SEQ = 8
ROWS = 1024
HROWS = 512
PAD = 16
NC = 3
CW = C // NC
MESH = pl.DeviceIdType.MESH
K0 = 0.7978845608028654
K1 = 0.044715
ORDER = (((2, 1), (2, 0)), ((1, 1), (3, 1)), ((1, 0), (3, 0)), ((0, 1), (0, 0)))


def gelu(x):
    return 0.5 * x * (1.0 + jnp.tanh(K0 * (x + K1 * (x * x * x))))


def gelu_both(x):
    square = x * x
    t = jnp.tanh(K0 * x * (1.0 + K1 * square))
    half = 0.5 * (1.0 + t)
    slope = half + 0.5 * x * (1.0 - t * t) * (K0 * (1.0 + 3.0 * K1 * square))
    return x * half, slope


def one_if(n):
    return jnp.clip(n, 0, 1).astype(jnp.float32)


def kernel(
    owner_ref, slot_ref, counts_ref, tokens_ref, dw_ref, down_ref, bdw_ref, bott_ref, cot_ref,
    owned_ref, out_ref, grad_ref,
    place_s, inv_s, tok, down, bott, cot, act_s, outgoing, qf, mixed, mixed_t, result,
    gbuf, csend, crecv, yacc, ysend, yrecv, zacc, zsend, zrecv, ssend, srecv,
    in_sem, halo_send, halo_recv, a_send, a_recv, own_sem, out_sem,
    c_send, c_recv, y_send, y_recv, z_send, z_recv, s_send, s_recv,
):
    dp = lax.axis_index("dp")
    me = lax.axis_index("seq")
    mx, mz = me // 2, me % 2
    core = dp % 2
    zh = (dp // 2) % 4
    my = dp // 8

    def seq_at(kx, kz):
        return ((mx + kx) % 4) * 2 + (mz + kz) % 2

    def dp_of(y, z, c):
        return y * 8 + z * 2 + c

    loads = [
        pltpu.make_async_copy(tokens_ref, tok.at[pl.ds(1, 64)], in_sem.at[0]),
        pltpu.make_async_copy(down_ref, down, in_sem.at[1]),
        pltpu.make_async_copy(bott_ref, bott, in_sem.at[2]),
        pltpu.make_async_copy(cot_ref.at[0], cot, in_sem.at[3]),
    ]
    for load in loads:
        load.start()

    barrier = pltpu.get_barrier_semaphore()
    peers = [(dp, seq_at(k // 2, k % 2)) for k in range(1, 8)]
    peers += [(dp_of(my, zh, 1 - core), me)]
    peers += [(dp_of((my + k) % 4, zh, core), me) for k in range(1, 4)]
    peers += [(dp_of(my, (zh + k) % 4, core), me) for k in range(1, 4)]
    for peer in peers:
        pl.semaphore_signal(barrier, inc=1, device_id=peer, device_id_type=MESH)

    def set_place(j, carry):
        place_s[j] = owner_ref[0, me * GROUPS_DEV + j] * CAP + slot_ref[0, me * GROUPS_DEV + j]
        return carry

    lax.fori_loop(0, GROUPS_DEV, set_place, 0)

    def set_inv(p, carry):
        found = jnp.int32(0)
        for j in range(GROUPS_DEV):
            found = found + j * (1 - jnp.minimum(jnp.abs(place_s[j] - p), 1))
        inv_s[p] = jnp.minimum(found, GROUPS_DEV - 1)
        return carry

    lax.fori_loop(0, GROUPS_DEV, set_inv, 0)
    ssend[...] = jnp.zeros_like(ssend)
    pl.semaphore_wait(barrier, len(peers))

    up, dn = (me + 1) % N_SEQ, (me + N_SEQ - 1) % N_SEQ
    halos = [
        pltpu.make_async_remote_copy(
            tokens_ref.at[63], tok.at[0],
            halo_send.at[0], halo_recv.at[0], device_id=(dp, up), device_id_type=MESH),
        pltpu.make_async_remote_copy(
            tokens_ref.at[0], tok.at[65],
            halo_send.at[1], halo_recv.at[1], device_id=(dp, dn), device_id_type=MESH),
    ]
    for h in halos:
        h.start()
    loads[0].wait()
    for h in halos:
        h.wait_recv()

    @pl.when(me == 0)
    def _():
        tok[0] = jnp.zeros((PAD, C), jnp.bfloat16)

    @pl.when(me == N_SEQ - 1)
    def _():
        tok[65] = jnp.zeros((PAD, C), jnp.bfloat16)

    w0, w1, w2 = dw_ref[0:1, :], dw_ref[1:2, :], dw_ref[2:3, :]
    my_count = counts_ref[0, me]

    def act_of(before, here, after):
        return here + gelu(w0 * before + w1 * here + w2 * after)

    def put_act(at, value):
        for b in range(6):
            act_s[b, pl.ds(at, value.shape[0]), :] = value[:, b * 128:b * 128 + 128]

    sends = []
    for step, pair in enumerate(ORDER):
        dests = [seq_at(*offset) for offset in pair]
        for n, dest in enumerate(dests):
            def one_group(slot, carry, n=n, dest=dest):
                group = inv_s[dest * CAP + slot]
                rows = tok[pl.ds(2 * group, 4)].reshape(2 * GROUP, C).astype(jnp.float32)
                put_act((n * CAP + slot) * GROUP, act_of(rows[8:40], rows[16:48], rows[24:56]))
                return carry

            lax.fori_loop(0, CAP, one_group, 0)
        last = step == len(ORDER) - 1
        if last:
            low = tok[0:2].reshape(GROUP, C).astype(jnp.float32)
            high = tok[64:66].reshape(GROUP, C).astype(jnp.float32)
            put_act(256, act_of(low[0:8], low[8:16], low[16:24]))
            put_act(264, act_of(high[8:16], high[16:24], high[24:32]))
            put_act(272, jnp.zeros((16, C), jnp.float32))
        m = 144 if last else 128
        even, odd = (
            jnp.concatenate([act_s[b, pl.ds(first, m, stride=2), :] for b in range(6)], axis=1)
            .astype(jnp.bfloat16)
            for first in (0, 1)
        )
        if step == 0:
            loads[1].wait()
        for nb in range(3):
            cols = pl.ds(nb * 512, 512)
            proj = jnp.dot(even, down[0:C, cols], preferred_element_type=jnp.float32)
            proj = proj + jnp.dot(odd, down[C:C2, cols], preferred_element_type=jnp.float32)
            panel = gelu(proj)
            for n, dest in enumerate(dests):
                for slot in range(CAP):
                    live = one_if(my_count - inv_s[dest * CAP + slot])
                    at = (n * CAP + slot) * HALF
                    outgoing[dest * CAP + slot, :, cols] = (
                        panel[at:at + HALF] * live).astype(jnp.bfloat16)
            if last:
                low_live = one_if(me) * one_if(counts_ref[0, (me + N_SEQ - 1) % N_SEQ] - (GROUPS_DEV - 1))
                high_live = one_if(N_SEQ - 1 - me) * one_if(counts_ref[0, (me + 1) % N_SEQ])
                ends = panel[128:136].astype(jnp.bfloat16).astype(jnp.float32)
                qf[4:8, cols] = ends[0:4] * low_live
                qf[520:524, cols] = ends[4:8] * high_live
        for n, (kx, kz) in enumerate(pair):
            src = outgoing.at[pl.ds(dests[n] * CAP, CAP)]
            dst = owned_ref.at[0, pl.ds(me * CAP, CAP)]
            if (kx, kz) == (0, 0):
                own = pltpu.make_async_copy(src, dst, own_sem)
                own.start()
            else:
                k = kx * 2 + kz - 1
                send = pltpu.make_async_remote_copy(
                    src, dst, a_send.at[k], a_recv.at[k],
                    device_id=(dp, dests[n]), device_id_type=MESH)
                send.start()
                sends.append(send)

    def place_rows(j, carry):
        qf[pl.ds(pl.multiple_of(8 + j * HALF, 8), HALF), :] = outgoing[place_s[j]].astype(jnp.float32)
        return carry

    lax.fori_loop(0, GROUPS_DEV, place_rows, 0)
    b0, b1, b2 = bdw_ref[0:1, :], bdw_ref[1:2, :], bdw_ref[2:3, :]

    def mix(r, carry):
        base = pl.multiple_of(r * 128, 128)
        for cb in range(6):
            cols = pl.ds(cb * 256, 256)
            v = qf[pl.ds(base, 144), cols]
            bb = slice(cb * 256, cb * 256 + 256)
            value = (b0[:, bb] * v[7:135] + b1[:, bb] * v[8:136] + b2[:, bb] * v[9:137])
            mixed[pl.ds(base, 128), cols] = value.astype(jnp.bfloat16)
            mixed_t[pl.ds(cb * 256, 256), pl.ds(base, 128)] = value.T.astype(jnp.bfloat16)
        return carry

    lax.fori_loop(0, 4, mix, 0)
    loads[2].wait()
    loads[3].wait()

    def copy_core(c):
        return pltpu.make_async_remote_copy(
            csend.at[c], crecv.at[c], c_send.at[c], c_recv.at[c],
            device_id=(dp_of(my, zh, 1 - core), me), device_id_type=MESH)

    def copy_y(c, k):
        return pltpu.make_async_remote_copy(
            ysend.at[c, k - 1], yrecv.at[c, k - 1], y_send.at[c, k - 1], y_recv.at[c, k - 1],
            device_id=(dp_of((my + k) % 4, zh, core), me), device_id_type=MESH)

    def copy_z(c, k):
        return pltpu.make_async_remote_copy(
            zsend.at[c, k - 1], zrecv.at[c, k - 1], z_send.at[c, k - 1], z_recv.at[c, k - 1],
            device_id=(dp_of(my, (zh + k) % 4, core), me), device_id_type=MESH)

    def copy_s(k):
        return pltpu.make_async_remote_copy(
            ssend.at[k], srecv.at[k - 1], s_send.at[k - 1], s_recv.at[k - 1],
            device_id=(dp, seq_at(k // 2, k % 2)), device_id_type=MESH)

    def make_term(c):
        cols = pl.ds(c * CW, CW)
        delta = []
        for r in range(4):
            rows = pl.ds(r * 128, 128)
            pre = jnp.dot(mixed[rows, :], bott[:, cols], preferred_element_type=jnp.float32)
            value, slope = gelu_both(pre)
            result[rows, cols] = value.astype(jnp.bfloat16)
            delta.append((cot[rows, cols].astype(jnp.float32) * slope).astype(jnp.bfloat16))
        delta = jnp.concatenate(delta, axis=0)
        for i in range(4):
            part = jnp.dot(mixed_t[pl.ds(i * 384, 384), :], delta, preferred_element_type=jnp.float32)
            gbuf[c, pl.ds(i * 4, 4)] = part.reshape(4, 2, 48, CW)
        csend[c] = gbuf[c, :, 1 - core].astype(jnp.bfloat16)
        copy_core(c).start()

    def after_core(c):
        copy_core(c).wait_recv()

        def summed(y):
            rows = pl.ds(y * 4, 4)
            return gbuf[c, rows, core] + crecv[c, rows].astype(jnp.float32)

        for k in (2, 1, 3):
            ysend[c, k - 1] = summed((my + k) % 4).astype(jnp.bfloat16)
            copy_y(c, k).start()
        yacc[c] = summed(my)

    def after_y(c):
        for k in (1, 2, 3):
            copy_y(c, k).wait_recv()

        def summed(z):
            total = yacc[c, z]
            for k in (1, 2, 3):
                total = total + yrecv[c, k - 1, z].astype(jnp.float32)
            return total

        for k in (2, 1, 3):
            zsend[c, k - 1] = summed((zh + k) % 4).astype(jnp.bfloat16)
            copy_z(c, k).start()
        zacc[:, pl.ds(c * CW, CW)] = summed(zh)

    def after_z(c):
        cols = pl.ds(c * CW, CW)
        total = zacc[:, cols]
        for k in (1, 2, 3):
            copy_z(c, k).wait_recv()
            total = total + zrecv[c, k - 1].astype(jnp.float32)
        for s in range(N_SEQ):
            sx, sz = s // 2, s % 2
            k = ((sx + 4 - mx) % 4) * 2 + (sz + 2 - mz) % 2
            ssend[k, 0:6, cols] = total[s * 6:s * 6 + 6]

    make_term(0)
    make_term(1)
    after_core(0)
    make_term(2)
    after_core(1)
    write = pltpu.make_async_copy(result, out_ref.at[0], out_sem)
    write.start()
    after_core(2)
    for c in range(NC):
        after_y(c)
    for c in range(NC):
        after_z(c)
    for k in (5, 4, 3, 7, 2, 6, 1):
        copy_s(k).start()
    total = ssend[0]
    for k in range(1, 8):
        copy_s(k).wait_recv()
        total = total + srecv[k - 1]
    grad_ref[...] = total[0:6]

    for send in sends:
        send.wait()
    own.wait()
    write.wait()
    for h in halos:
        h.wait_send()
    for c in range(NC):
        copy_core(c).wait_send()
        for k in (1, 2, 3):
            copy_y(c, k).wait_send()
            copy_z(c, k).wait_send()
    for k in range(1, 8):
        copy_s(k).wait_send()


def on_device(tokens, depthwise_weight, down_weight, bott_dw, bott_weight, cotangent,
              plan_owner, plan_slot, counts):
    smem = pl.BlockSpec(memory_space=pltpu.SMEM)
    vmem = pl.BlockSpec(memory_space=pltpu.VMEM)
    far = pl.BlockSpec(memory_space=pl.ANY)
    bf16, f32 = jnp.bfloat16, jnp.float32
    V, DMA = pltpu.VMEM, pltpu.SemaphoreType.DMA
    return pl.pallas_call(
        kernel,
        out_shape=(
            jax.ShapeDtypeStruct((1, GROUPS_DEV, HALF, C2), bf16),
            jax.ShapeDtypeStruct((1, HROWS, C), bf16),
            jax.ShapeDtypeStruct((6, C), f32),
        ),
        in_specs=[smem, smem, smem, far, vmem, far, vmem, far, far],
        out_specs=(far, far, vmem),
        scratch_shapes=[
            pltpu.SMEM((GROUPS_DEV,), jnp.int32),
            pltpu.SMEM((GROUPS_DEV,), jnp.int32),
            V((ROWS // PAD + 2, PAD, C), bf16),
            V((C2, C2), bf16),
            V((C2, C), bf16),
            V((HROWS, C), bf16),
            V((6, 288, 128), f32),
            V((GROUPS_DEV, HALF, C2), bf16),
            V((HROWS + 16, C2), f32),
            V((HROWS, C2), bf16),
            V((C2, HROWS), bf16),
            V((HROWS, C), bf16),
            V((NC, 16, 2, 48, CW), f32),
            V((NC, 16, 48, CW), bf16),
            V((NC, 16, 48, CW), bf16),
            V((NC, 4, 48, CW), f32),
            V((NC, 3, 4, 48, CW), bf16),
            V((NC, 3, 4, 48, CW), bf16),
            V((48, C), f32),
            V((NC, 3, 48, CW), bf16),
            V((NC, 3, 48, CW), bf16),
            V((8, 8, C), f32),
            V((7, 8, C), f32),
            DMA((4,)), DMA((2,)), DMA((2,)), DMA((7,)), DMA((7,)), DMA, DMA,
            DMA((NC,)), DMA((NC,)), DMA((NC, 3)), DMA((NC, 3)),
            DMA((NC, 3)), DMA((NC, 3)), DMA((7,)), DMA((7,)),
        ],
        compiler_params=pltpu.CompilerParams(
            collective_id=0, has_side_effects=True, vmem_limit_bytes=56 * 1024 * 1024),
        cost_estimate=pl.CostEstimate(
            flops=5_000_000_000, bytes_accessed=14_000_000, transcendentals=2_000_000),
    )(plan_owner, plan_slot, counts, tokens.reshape(ROWS // PAD, PAD, C), depthwise_weight, down_weight, bott_dw,
      bott_weight, cotangent)


def solution(mesh):
    placed = (
        P("dp", "seq", None),
        P(),
        P(),
        P(),
        P(),
        P("dp", "seq", None),
        P("dp", None),
        P("dp", None),
        P("dp", None),
    )
    return jax.shard_map(
        on_device,
        mesh=mesh,
        in_specs=placed,
        out_specs=(P("dp", "seq", None, None), P("dp", "seq", None), P(("dp", "seq"), None)),
        check_vma=False,
    )
```

time: 626 us -> 56.3 us (0.09)
  waiting for transfers between devices: 524 us -> 0 us
  Pallas kernels: 0 us -> 51.2 us
  blocking collectives: 25.1 us -> 0 us
  local copies, waits for them, and re-layouts: 23.7 us -> 4.22 us
  matrix products: 15 us -> 0 us
  between operations: 14.3 us -> 0.66 us
  starting transfers between devices: 11.9 us -> 0 us
  other arithmetic: 11.3 us -> 0 us
    psum x1 -> x0, waiting for transfers between devices: 270 us -> none  [on_device(): summed = lax.psum(term, ('dp', 'seq'))]
    all_gather x1 -> x0, waiting for transfers between devices: 250 us -> none  [on_device(): everything = lax.all_gather(owned, 'seq', axis=1, tiled=True)]
    pallas_call x0 -> x1, Pallas kernels: none -> 51.2 us  [on_device(): pl.pallas_call(kernel, out_shape=(jax.ShapeDtypeStruct((1, GROUPS_DEV, HA...]
    all_to_all x1 -> x0, blocking collectives: 25.1 us -> none  [on_device(): lax.all_to_all(outgoing, 'seq', split_axis=1, concat_axis=1, tiled=True)]
    dot_general x4 -> x0, matrix products: 15 us -> none  [the longest x1 7.03 us: on_device(): jnp.einsum('wnkhd,de->wnkhe', pairs, down_weight, preferred_element_type=...]
    ppermute x4 -> x0, starting transfers between devices: 11.9 us -> none  [the longest x2 7.06 us: padded(): lax.ppermute(lax.slice_in_dim(block, 0, width, axis=dim), axis, backward)]
    convert_element_type x4 -> x0, other arithmetic: 6.77 us -> none  [the longest x1 2.78 us: on_device(): return (owned, result.astype(jnp.bfloat16), grad_rows)]
    gather x1 -> x0, local copies, waits for them, and re-layouts: 6.42 us -> none  [on_device(): mine = jnp.take_along_axis(everything, mine_index[:, :, None, None], axis=1)]
  transfers between devices with their start and end apart: 6 -> 0, of which waited for: 4 -> 0; matrix products, arithmetic and copies ran while one was open for 1% -> 0% of each run, Pallas kernels for 0% -> 0%
where the time goes in v1:
time: 56.3 us; the launch traced here: 56.1 us
  Pallas kernels  51.2 us (91%)
  local copies, waits for them, and re-layouts  4.22 us (7%)
  between operations  0.66 us (1%)
    pallas_call x1, Pallas kernels, on_device(): pl.pallas_call(kernel, out_shape=(jax.ShapeDtypeStruct((1, GROUPS_DEV, HA...  51.2 us
    unnamed x7, local copies, waits for them, and re-layouts  4.22 us

profile of v1, /device:TPU:2, one launch (start us, length us, event | category | flops | bytes accessed | tf_op | source)
XLA Modules:
  0.0 56.1 jit_solution(3525887697076434421)
XLA Ops:
  0.6 51.2 %shard_map.112 = (bf16[1,32,16,1536]{3,2,1,0:T(8,128)(2,1)}, bf16[1,512,768]{2,1,0:T(8,128)(2,1)}, f32[6,768]{1,0:T(8,128)}) custom-call(s32[1,256]{1,0:T(1,128)} %owner_ref.1, s32[1,256]{1,0:T(1,128)} %slot_ref.1, s32[1,8]{1,0:T(1,128)} %counts_ref.1, bf16[64,16,768]{2,1,0:T(8,128)(2,1)} %bitcast.1, f32[3,768]{1,0:T(4,128)} %dw_ref.1, ...), custom_call_target="tpu_custom_call" | custom-call | flops 5000000000 | bytes 14000000 | tf_op jit(solution)/shard_map/pallas_call | solution.py:325
  51.9 0.0 copy-start
  51.9 0.0 copy-start.1
  51.9 2.7 %copy.15 = bf16[1,32,16,1536]{3,2,1,0:T(8,128)(2,1)} copy(bf16[1,32,16,1536]{3,2,1,0:T(8,128)(2,1)} %get-tuple-element.6) | data formatting | bytes 3145728
  54.6 0.0 copy-done
  54.6 0.9 %copy.16 = bf16[1,512,768]{2,1,0:T(8,128)(2,1)} copy(bf16[1,512,768]{2,1,0:T(8,128)(2,1)S(1)} %copy-done) | data formatting | bytes 1572864
  55.5 0.0 copy-done.1
  55.5 0.6 %copy.17 = f32[6,768]{1,0:T(8,128)} copy(f32[6,768]{1,0:T(8,128)S(1)} %copy-done.1) | data formatting | bytes 36864
Async XLA Ops:
  51.9 2.7 %copy-start = (bf16[1,512,768]{2,1,0:T(8,128)(2,1)S(1)}, bf16[1,512,768]{2,1,0:T(8,128)(2,1)}, u32[]{:S(2)}) copy-start(bf16[1,512,768]{2,1,0:T(8,128)(2,1)} %get-tuple-element.7) | copy-start | bytes 2359300
  51.9 3.6 %copy-start.1 = (f32[6,768]{1,0:T(8,128)S(1)}, f32[6,768]{1,0:T(8,128)}, u32[]{:S(2)}) copy-start(f32[6,768]{1,0:T(8,128)} %get-tuple-element.8) | copy-start | bytes 55300

commit v2 on v1

v2 whole, which is shorter than its diff:
```python
import jax
import jax.numpy as jnp
from jax import lax
from jax.experimental import pallas as pl
from jax.experimental.pallas import tpu as pltpu
from jax.sharding import PartitionSpec as P

C = 768
C2 = 1536
GROUP = 32
GROUPS_DEV = 32
HALF = 16
CAP = 4
N_SEQ = 8
ROWS = 1024
HROWS = 512
PAD = 16
NC = 3
CW = C // NC
MESH = pl.DeviceIdType.MESH
K0 = 0.7978845608028654
K1 = 0.044715
ORDER = (((2, 1), (2, 0)), ((1, 1), (3, 1)), ((1, 0), (3, 0)), ((0, 1), (0, 0)))
BF16, F32 = jnp.bfloat16, jnp.float32


def gelu(x):
    return 0.5 * x * (1.0 + jnp.tanh(K0 * x * (1.0 + K1 * (x * x))))


def gelu_both(x):
    square = x * x
    t = jnp.tanh(K0 * x * (1.0 + K1 * square))
    half = 0.5 * (1.0 + t)
    slope = half + 0.5 * x * (1.0 - t * t) * (K0 * (1.0 + 3.0 * K1 * square))
    return x * half, slope


def one_if(n):
    return jnp.clip(n, 0, 1).astype(F32)


def pack24(v):
    rest = v[16:24]
    return jnp.concatenate(
        [v[0:16], jnp.concatenate([rest[:, 0:128], rest[:, 128:256]], axis=0)], axis=1)


def unpack24(v):
    rest = v[:, 256:384]
    return jnp.concatenate(
        [v[:, 0:256], jnp.concatenate([rest[0:8], rest[8:16]], axis=1)], axis=0)


def pack8(v):
    return jnp.concatenate([v[:, 0:128], v[:, 128:256]], axis=0)


def unpack8(v):
    return jnp.concatenate([v[0:8], v[8:16]], axis=1)


def kernel(
    owner_ref, slot_ref, counts_ref, tokens_ref, dw_ref, down_ref, bdw_ref, bott_ref, cot_ref,
    owned_ref, out_ref, grad_ref,
    owner_s, slot_s, counts_s, place_s, inv_s, dw, bdw,
    tok, halo, down, bott, cot, act_s, pairs, outgoing, qf, mixed, mixed_t, result,
    gbuf, csend, crecv, bown, ysend, yrecv, sown, ssend, srecv, zown, zsend, zrecv,
    in_sem, halo_send, halo_recv, a_send, a_recv, own_sem, out_sem,
    c_send, c_recv, y_send, y_recv, s_send, s_recv, z_send, z_recv,
):
    dp = lax.axis_index("dp")
    me = lax.axis_index("seq")
    mx, mz = me // 2, me % 2
    core = dp % 2
    zh = (dp // 2) % 4
    my = dp // 8

    def seq_at(kx, kz):
        return ((mx + kx) % 4) * 2 + (mz + kz) % 2

    def dp_of(y, z, c):
        return y * 8 + z * 2 + c

    barrier = pltpu.get_barrier_semaphore()
    peers = [(dp, seq_at(k // 2, k % 2)) for k in range(1, 8)]
    peers += [(dp_of(my, zh, 1 - core), me)]
    peers += [(dp_of((my + k) % 4, zh, core), me) for k in (1, 3)]
    peers += [(dp_of(my, (zh + k) % 4, core), me) for k in range(1, 4)]
    for peer in peers:
        pl.semaphore_signal(barrier, inc=1, device_id=peer, device_id_type=MESH)

    loads = [
        pltpu.make_async_copy(src, dst, in_sem.at[i])
        for i, (src, dst) in enumerate((
            (tokens_ref, tok.at[pl.ds(1, 64)]), (dw_ref, dw), (owner_ref, owner_s), (slot_ref, slot_s),
            (counts_ref, counts_s), (down_ref, down), (bdw_ref, bdw), (bott_ref, bott), (cot_ref.at[0], cot),
        ))
    ]
    for load in loads:
        load.start()
    tok[0] = jnp.zeros((PAD, C), BF16)
    tok[65] = jnp.zeros((PAD, C), BF16)
    pl.semaphore_wait(barrier, len(peers))

    up, dn = (me + 1) % N_SEQ, (me + N_SEQ - 1) % N_SEQ
    halos = [
        pltpu.make_async_remote_copy(
            tokens_ref.at[63], halo.at[0],
            halo_send.at[0], halo_recv.at[0], device_id=(dp, up), device_id_type=MESH),
        pltpu.make_async_remote_copy(
            tokens_ref.at[0], halo.at[1],
            halo_send.at[1], halo_recv.at[1], device_id=(dp, dn), device_id_type=MESH),
    ]
    for h in halos:
        h.start()
    loads[0].wait()
    loads[1].wait()

    def act_of(rows, count, b):
        cols = slice(b * 128, b * 128 + 128)
        here = rows[8:8 + count, cols]
        conv = (dw[0:1, cols] * rows[0:count, cols] + dw[1:2, cols] * here
                + dw[2:3, cols] * rows[16:16 + count, cols])
        return here + gelu(conv)

    def paired(at, count, first):
        return jnp.concatenate(
            [act_s[at, b, pl.ds(first + odd, count, stride=2), :] for odd in (0, 1) for b in range(6)],
            axis=1).astype(BF16)

    def four_groups(i, carry):
        rows = tok[pl.ds(8 * i, 10)].reshape(160, C).astype(F32)[8:152]
        for b in range(6):
            act_s[0, b, 0:128, :] = act_of(rows, 128, b)
        pairs[pl.ds(4 * i, 4)] = paired(0, 64, 0).reshape(4, HALF, C2)
        return carry

    lax.fori_loop(0, 8, four_groups, 0)

    for load in loads[2:5]:
        load.wait()

    def set_place(j, carry):
        place_s[j] = owner_s[0, me * GROUPS_DEV + j] * CAP + slot_s[0, me * GROUPS_DEV + j]
        return carry

    lax.fori_loop(0, GROUPS_DEV, set_place, 0)

    def set_inv(p, carry):
        found = jnp.int32(0)
        for j in range(GROUPS_DEV):
            found = found + j * (1 - jnp.minimum(jnp.abs(place_s[j] - p), 1))
        inv_s[p] = jnp.minimum(found, GROUPS_DEV - 1)
        return carry

    lax.fori_loop(0, GROUPS_DEV, set_inv, 0)

    for h in halos:
        h.wait_recv()
    low = jnp.concatenate(
        [halo[0].astype(F32) * one_if(me), tok[1:4].reshape(48, C).astype(F32)], axis=0)
    high = jnp.concatenate(
        [tok[62:65].reshape(48, C).astype(F32), halo[1].astype(F32) * one_if(N_SEQ - 1 - me)], axis=0)
    for b in range(6):
        act_s[0, b, 0:40, :] = act_of(low, 40, b)
        act_s[1, b, 0:40, :] = act_of(high[8:64], 40, b)
    pairs[0] = paired(0, 16, 8)
    pairs[GROUPS_DEV - 1] = paired(1, 16, 0)
    zero = jnp.zeros((8, C2), BF16)
    ends = jnp.concatenate([paired(0, 4, 0), paired(1, 4, 32), zero], axis=0)

    my_count = counts_s[0, me]
    sends = []
    for step, pair in enumerate(ORDER):
        dests = [seq_at(*offset) for offset in pair]
        groups = [inv_s[dest * CAP + slot] for dest in dests for slot in range(CAP)]
        places = [dest * CAP + slot for dest in dests for slot in range(CAP)]
        last = step == len(ORDER) - 1
        rows = jnp.concatenate([pairs[group] for group in groups] + ([ends] if last else []), axis=0)
        if step == 0:
            loads[5].wait()
        for nb in range(3):
            cols = pl.ds(nb * 512, 512)
            panel = gelu(jnp.dot(rows, down[:, cols], preferred_element_type=F32))
            for n in range(8):
                live = one_if(my_count - groups[n])
                outgoing[places[n], :, cols] = (panel[n * HALF:n * HALF + HALF] * live).astype(BF16)
            if last:
                low_live = one_if(me) * one_if(counts_s[0, dn] - (GROUPS_DEV - 1))
                high_live = one_if(N_SEQ - 1 - me) * one_if(counts_s[0, up])
                beyond = panel[128:136].astype(BF16).astype(F32)
                qf[4:8, cols] = beyond[0:4] * low_live
                qf[520:524, cols] = beyond[4:8] * high_live
        for n, (kx, kz) in enumerate(pair):
            src = outgoing.at[pl.ds(dests[n] * CAP, CAP)]
            dst = owned_ref.at[0, pl.ds(me * CAP, CAP)]
            if (kx, kz) == (0, 0):
                own = pltpu.make_async_copy(src, dst, own_sem)
                own.start()
            else:
                k = kx * 2 + kz - 1
                send = pltpu.make_async_remote_copy(
                    src, dst, a_send.at[k], a_recv.at[k],
                    device_id=(dp, dests[n]), device_id_type=MESH)
                send.start()
                sends.append(send)

    def place_rows(j, carry):
        qf[pl.ds(pl.multiple_of(8 + j * HALF, 8), HALF), :] = outgoing[place_s[j]].astype(F32)
        return carry

    lax.fori_loop(0, GROUPS_DEV, place_rows, 0)
    loads[6].wait()

    def mix(r, carry):
        base = pl.multiple_of(r * 128, 128)
        for cb in range(6):
            cols = pl.ds(cb * 256, 256)
            v = qf[pl.ds(base, 144), cols]
            value = bdw[0:1, cols] * v[7:135] + bdw[1:2, cols] * v[8:136] + bdw[2:3, cols] * v[9:137]
            mixed[pl.ds(base, 128), cols] = value.astype(BF16)
            mixed_t[pl.ds(cb * 256, 256), pl.ds(base, 128)] = value.T.astype(BF16)
        return carry

    lax.fori_loop(0, 4, mix, 0)
    loads[7].wait()
    loads[8].wait()

    def remote(src, dst, send_sem, recv_sem, device):
        return pltpu.make_async_remote_copy(
            src, dst, send_sem, recv_sem, device_id=device, device_id_type=MESH)

    def copy_core(c):
        return remote(csend.at[c], crecv.at[c], c_send.at[c], c_recv.at[c], (dp_of(my, zh, 1 - core), me))

    def copy_y(c, n):
        to = (my + (1 if n < 3 else 3)) % 4
        return remote(ysend.at[c, n], yrecv.at[c, n], y_send.at[c, n], y_recv.at[c, n],
                      (dp_of(to, zh, core), me))

    def copy_s(c, k):
        return remote(ssend.at[c, k], srecv.at[c, k - 1], s_send.at[c, k - 1], s_recv.at[c, k - 1],
                      (dp, seq_at(k // 2, k % 2)))

    def copy_z(c, k):
        return remote(zsend.at[c, k], zrecv.at[c, k - 1], z_send.at[c, k - 1], z_recv.at[c, k - 1],
                      (dp_of(my, (zh + k) % 4, core), me))

    def make_term(c):
        cols = pl.ds(c * CW, CW)
        delta = []
        for r in range(4):
            rows = pl.ds(r * 128, 128)
            pre = jnp.dot(mixed[rows, :], bott[:, cols], preferred_element_type=F32)
            value, slope = gelu_both(pre)
            result[rows, cols] = value.astype(BF16)
            delta.append((cot[rows, cols].astype(F32) * slope).astype(BF16))
        delta = jnp.concatenate(delta, axis=0)
        for i in range(4):
            part = jnp.dot(mixed_t[pl.ds(i * 384, 384), :], delta, preferred_element_type=F32)
            gbuf[c, pl.ds(i * 4, 4)] = part.reshape(4, 2, 48, CW)
        csend[c] = gbuf[c, :, 1 - core].astype(BF16)
        copy_core(c).start()

    def after_core(c):
        copy_core(c).wait_recv()

        def summed(y, half):
            rows = pl.ds(y * 4 + half * 2, 2)
            return gbuf[c, rows, core] + crecv[c, rows].astype(F32)

        nxt, across, prv = (my + 1) % 4, (my + 2) % 4, (my + 3) % 4
        for n, block, half in ((0, across, 0), (3, across, 1), (1, nxt, 1), (4, prv, 0)):
            ysend[c, n] = summed(block, half).astype(BF16)
            copy_y(c, n).start()
        bown[c, 0] = summed(nxt, 0)
        bown[c, 1] = summed(prv, 1)
        bown[c, 2] = summed(my, 0)
        bown[c, 3] = summed(my, 1)

    def pass_y(c):
        copy_y(c, 0).wait_recv()
        ysend[c, 2] = (bown[c, 0] + yrecv[c, 0].astype(F32)).astype(BF16)
        copy_y(c, 2).start()
        copy_y(c, 3).wait_recv()
        ysend[c, 5] = (bown[c, 1] + yrecv[c, 3].astype(F32)).astype(BF16)
        copy_y(c, 5).start()

    def after_y(c):
        for n in (1, 4, 2, 5):
            copy_y(c, n).wait_recv()
        half0 = bown[c, 2] + yrecv[c, 2].astype(F32) + yrecv[c, 4].astype(F32)
        half1 = bown[c, 3] + yrecv[c, 1].astype(F32) + yrecv[c, 5].astype(F32)
        blocks = (half0[0], half0[1], half1[0], half1[1])
        for s in range(N_SEQ):
            k = ((s // 2 + 4 - mx) % 4) * 2 + (s % 2 + 2 - mz) % 2
            part = jnp.concatenate([block[s * 6:s * 6 + 6] for block in blocks], axis=0)
            part = pack24(part)
            sown[c, k] = part
            ssend[c, k] = part.astype(BF16)
        for k in (5, 4, 3, 7, 2, 6, 1):
            copy_s(c, k).start()

    def after_s(c):
        total = sown[c, 0]
        for k in range(1, 8):
            copy_s(c, k).wait_recv()
            total = total + srecv[c, k - 1].astype(F32)
        total = unpack24(total)
        for z in range(4):
            k = (z + 4 - zh) % 4
            part = jnp.concatenate([total[z * 6:z * 6 + 6], jnp.zeros((2, CW), F32)], axis=0)
            zown[c, k] = part
            zsend[c, k] = pack8(part).astype(BF16)
        for k in (2, 1, 3):
            copy_z(c, k).start()

    def after_z(c):
        total = zown[c, 0]
        for k in (1, 2, 3):
            copy_z(c, k).wait_recv()
            total = total + unpack8(zrecv[c, k - 1].astype(F32))
        grad_ref[:, c * CW:c * CW + CW] = total[0:6]

    make_term(0)
    make_term(1)
    after_core(0)
    make_term(2)
    after_core(1)
    pass_y(0)
    write = pltpu.make_async_copy(result, out_ref.at[0], out_sem)
    write.start()
    after_core(2)
    pass_y(1)
    after_y(0)
    pass_y(2)
    after_y(1)
    after_s(0)
    after_y(2)
    after_s(1)
    after_s(2)
    for c in range(NC):
        after_z(c)

    for send in sends:
        send.wait()
    own.wait()
    write.wait()
    for h in halos:
        h.wait_send()
    for c in range(NC):
        copy_core(c).wait_send()
        for n in range(6):
            copy_y(c, n).wait_send()
        for k in range(1, 8):
            copy_s(c, k).wait_send()
        for k in range(1, 4):
            copy_z(c, k).wait_send()


OUTS = (
    jax.ShapeDtypeStruct((1, GROUPS_DEV, HALF, C2), BF16),
    jax.ShapeDtypeStruct((1, HROWS, C), BF16),
    jax.ShapeDtypeStruct((6, C), F32),
)
FAR = pl.BlockSpec(memory_space=pl.ANY)


def hand_over(owned_ref, out_ref, grad_ref, owned_to, out_to, grad_to, sems):
    copies = [pltpu.make_async_copy(grad_ref, grad_to, sems.at[0])]
    for i in range(4):
        rows = pl.ds(i * 8, 8)
        copies.append(pltpu.make_async_copy(owned_ref.at[0, rows], owned_to.at[0, rows], sems.at[1 + i]))
    for i in range(2):
        rows = pl.ds(i * 256, 256)
        copies.append(pltpu.make_async_copy(out_ref.at[0, rows], out_to.at[0, rows], sems.at[5 + i]))
    for copy in copies:
        copy.start()
    for copy in copies:
        copy.wait()


def on_device(tokens, depthwise_weight, down_weight, bott_dw, bott_weight, cotangent,
              plan_owner, plan_slot, counts):
    V, S, DMA = pltpu.VMEM, pltpu.SMEM, pltpu.SemaphoreType.DMA
    made = pl.pallas_call(
        kernel,
        out_shape=tuple(pltpu.VMEM(o.shape, o.dtype) for o in OUTS),
        in_specs=[FAR] * 9,
        out_specs=(pl.BlockSpec(memory_space=pltpu.VMEM),) * 3,
        scratch_shapes=[
            S((1, 256), jnp.int32),
            S((1, 256), jnp.int32),
            S((1, 8), jnp.int32),
            S((GROUPS_DEV,), jnp.int32),
            S((GROUPS_DEV,), jnp.int32),
            V((3, C), F32),
            V((3, C2), F32),
            V((ROWS // PAD + 2, PAD, C), BF16),
            V((2, PAD, C), BF16),
            V((C2, C2), BF16),
            V((C2, C), BF16),
            V((HROWS, C), BF16),
            V((2, 6, 128, 128), F32),
            V((GROUPS_DEV, HALF, C2), BF16),
            V((GROUPS_DEV, HALF, C2), BF16),
            V((HROWS + 16, C2), F32),
            V((HROWS, C2), BF16),
            V((C2, HROWS), BF16),
            V((HROWS, C), BF16),
            V((NC, 16, 2, 48, CW), F32),
            V((NC, 16, 48, CW), BF16),
            V((NC, 16, 48, CW), BF16),
            V((NC, 4, 2, 48, CW), F32),
            V((NC, 6, 2, 48, CW), BF16),
            V((NC, 6, 2, 48, CW), BF16),
            V((NC, 8, 16, 384), F32),
            V((NC, 8, 16, 384), BF16),
            V((NC, 7, 16, 384), BF16),
            V((NC, 4, 8, CW), F32),
            V((NC, 4, 16, 128), BF16),
            V((NC, 3, 16, 128), BF16),
            DMA((9,)), DMA((2,)), DMA((2,)), DMA((7,)), DMA((7,)), DMA, DMA,
            DMA((NC,)), DMA((NC,)), DMA((NC, 6)), DMA((NC, 6)),
            DMA((NC, 7)), DMA((NC, 7)), DMA((NC, 3)), DMA((NC, 3)),
        ],
        compiler_params=pltpu.CompilerParams(
            collective_id=0, has_side_effects=True, vmem_limit_bytes=56 * 1024 * 1024),
        cost_estimate=pl.CostEstimate(
            flops=5_000_000_000, bytes_accessed=14_000_000, transcendentals=2_000_000),
    )(plan_owner, plan_slot, counts, tokens.reshape(ROWS // PAD, PAD, C), depthwise_weight, down_weight,
      bott_dw, bott_weight, cotangent)
    return pl.pallas_call(
        hand_over,
        out_shape=OUTS,
        in_specs=[FAR] * 3,
        out_specs=(FAR,) * 3,
        scratch_shapes=[DMA((7,))],
        compiler_params=pltpu.CompilerParams(vmem_limit_bytes=40 * 1024 * 1024),
    )(*made)


def solution(mesh):
    placed = (
        P("dp", "seq", None),
        P(),
        P(),
        P(),
        P(),
        P("dp", "seq", None),
        P("dp", None),
        P("dp", None),
        P("dp", None),
    )
    return jax.shard_map(
        on_device,
        mesh=mesh,
        in_specs=placed,
        out_specs=(P("dp", "seq", None, None), P("dp", "seq", None), P(("dp", "seq"), None)),
        check_vma=False,
    )
```

time: 56.3 us -> 47.3 us (0.84)
  Pallas kernels: 51.2 us -> 46.5 us
  local copies, waits for them, and re-layouts: 4.22 us -> 0 us
    pallas_call x1 -> x2, Pallas kernels: 51.2 us -> 46.5 us  [the longest x1 45.1 us: on_device(): pl.pallas_call(kernel, out_shape=tuple((pltpu.VMEM(o.shape, o.dtype) for...]
    unnamed x7 -> x0, local copies, waits for them, and re-layouts: 4.22 us -> none
where the time goes in v2:
time: 47.3 us; the launch traced here: 47.2 us
  Pallas kernels  46.5 us (98%)
  between operations  0.64 us (1%)
    pallas_call x1, Pallas kernels, on_device(): pl.pallas_call(kernel, out_shape=tuple((pltpu.VMEM(o.shape, o.dtype) for...  45.1 us
    pallas_call x1, Pallas kernels, on_device(): pl.pallas_call(hand_over, out_shape=OUTS, in_specs=[FAR] * 3, out_specs=(...  1.46 us

profile of v2, /device:TPU:2, one launch (start us, length us, event | category | flops | bytes accessed | tf_op | source)
XLA Modules:
  0.0 47.2 jit_solution(9287772599787674272)
XLA Ops:
  0.6 45.1 %shard_map.112 = (bf16[1,32,16,1536]{3,2,1,0:T(8,128)(2,1)S(1)}, bf16[1,512,768]{2,1,0:T(8,128)(2,1)S(1)}, f32[6,768]{1,0:T(8,128)S(1)}) custom-call(s32[1,256]{1,0:T(1,128)} %owner_ref.1, s32[1,256]{1,0:T(1,128)} %slot_ref.1, s32[1,8]{1,0:T(1,128)} %counts_ref.1, bf16[64,16,768]{2,1,0:T(8,128)(2,1)} %bitcast.1, f32[3,768]{1,0:T(4,128)} %dw_ref.1, ...), custom_call_target="tpu_custom_call" | custom-call | flops 5000000000 | bytes 14000000 | tf_op jit(solution)/shard_map/pallas_call | solution.py:387
  45.7 1.5 %shard_map.113 = (bf16[1,32,16,1536]{3,2,1,0:T(8,128)(2,1)}, bf16[1,512,768]{2,1,0:T(8,128)(2,1)}, f32[6,768]{1,0:T(8,128)}) custom-call(bf16[1,32,16,1536]{3,2,1,0:T(8,128)(2,1)S(1)} %get-tuple-element.6.owned_ref, bf16[1,512,768]{2,1,0:T(8,128)(2,1)S(1)} %get-tuple-element.7.out_ref, f32[6,768]{1,0:T(8,128)S(1)} %get-tuple-element.8.grad_ref), custom_call_target="tpu_custom_call" | custom-call | tf_op jit(solution)/shard_map/pallas_call | solution.py:434

commit v3 on v2

v3 whole, which is shorter than its diff:
```python
import jax
import jax.numpy as jnp
from jax import lax
from jax.experimental import pallas as pl
from jax.experimental.pallas import tpu as pltpu
from jax.sharding import PartitionSpec as P

C = 768
C2 = 1536
GROUP = 32
GROUPS_DEV = 32
HALF = 16
CAP = 4
N_SEQ = 8
ROWS = 1024
HROWS = 512
PAD = 16
NC = 3
CW = C // NC
MESH = pl.DeviceIdType.MESH
K0 = 0.7978845608028654
K1 = 0.044715
ORDER = (((2, 1), (1, 1), (3, 1), (0, 1), (2, 0), (1, 0), (3, 0), (0, 0)), (), (), (), ())
BF16, F32 = jnp.bfloat16, jnp.float32


def gelu(x):
    return 0.5 * x * (1.0 + jnp.tanh(K0 * x * (1.0 + K1 * (x * x))))


def gelu_both(x):
    square = x * x
    t = jnp.tanh(K0 * x * (1.0 + K1 * square))
    half = 0.5 * (1.0 + t)
    slope = half + 0.5 * x * (1.0 - t * t) * (K0 * (1.0 + 3.0 * K1 * square))
    return x * half, slope


def one_if(n):
    return jnp.clip(n, 0, 1).astype(F32)


def pack8(v):
    v = jnp.concatenate([v, jnp.zeros((2, v.shape[1]), F32)], axis=0)
    if v.shape[1] == 128:
        return jnp.concatenate([v, jnp.zeros((8, 128), F32)], axis=0)
    return jnp.concatenate([v[:, 0:128], v[:, 128:256]], axis=0)


def unpack8(v, width):
    if width == 128:
        return v[0:6]
    return jnp.concatenate([v[0:6], v[8:14]], axis=1)


def kernel(
    owner_ref, slot_ref, counts_ref, tokens_ref, dw_ref, down_ref, bdw_ref, bott_ref, cot_ref,
    owned_ref, out_ref, grad_ref,
    owner_s, slot_s, counts_s, amount_s, inv_s, dw, bdw,
    tok, halo, down, bott, cot, act_s, pairs, panels, outgoing, qf, mixed, mixed_t,
    gbuf, csend, crecv, chunk_bufs,
    in_sem, halo_send, halo_recv, a_send, a_recv, own_sem,
    c_send, c_recv, chunk_sems,
):
    dp = lax.axis_index("dp")
    me = lax.axis_index("seq")
    mx, mz = me // 2, me % 2
    core = dp % 2
    zh = (dp // 2) % 4
    my = dp // 8

    def seq_at(kx, kz):
        return ((mx + kx) % 4) * 2 + (mz + kz) % 2

    def dp_of(y, z, c):
        return y * 8 + z * 2 + c

    loads = [
        pltpu.make_async_copy(src, dst, in_sem.at[i])
        for i, (src, dst) in enumerate((
            (tokens_ref, tok.at[pl.ds(1, 64)]), (dw_ref, dw), (owner_ref, owner_s), (slot_ref, slot_s),
            (counts_ref, counts_s), (down_ref, down), (bdw_ref, bdw), (bott_ref, bott), (cot_ref.at[0], cot),
        ))
    ]
    for load in loads[0:6]:
        load.start()
    barrier = pltpu.get_barrier_semaphore()
    peers = [(dp, seq_at(k // 2, k % 2)) for k in range(1, 8)]
    peers += [(dp_of(my, zh, 1 - core), me)]
    peers += [(dp_of((my + k) % 4, zh, core), me) for k in range(1, 4)]
    peers += [(dp_of(my, (zh + k) % 4, core), mx * 2 + z) for k in range(1, 4) for z in range(2)]
    for peer in peers:
        pl.semaphore_signal(barrier, inc=1, device_id=peer, device_id_type=MESH)

    tok[0] = jnp.zeros((PAD, C), BF16)
    tok[65] = jnp.zeros((PAD, C), BF16)
    pl.semaphore_wait(barrier, len(peers))

    up, dn = (me + 1) % N_SEQ, (me + N_SEQ - 1) % N_SEQ
    halos = [
        pltpu.make_async_remote_copy(
            tokens_ref.at[63], halo.at[0],
            halo_send.at[0], halo_recv.at[0], device_id=(dp, up), device_id_type=MESH),
        pltpu.make_async_remote_copy(
            tokens_ref.at[0], halo.at[1],
            halo_send.at[1], halo_recv.at[1], device_id=(dp, dn), device_id_type=MESH),
    ]
    for h in halos:
        h.start()

    loads[0].wait()
    loads[1].wait()

    def act_of(rows, count, b):
        cols = slice(b * 128, b * 128 + 128)
        here = rows[8:8 + count, cols]
        conv = (dw[0:1, cols] * rows[0:count, cols] + dw[1:2, cols] * here
                + dw[2:3, cols] * rows[16:16 + count, cols])
        return here + gelu(conv)

    def paired(at, count, first):
        return jnp.concatenate(
            [act_s[at, b, pl.ds(first + odd, count, stride=2), :] for odd in (0, 1) for b in range(6)],
            axis=1).astype(BF16)

    def four_groups(i):
        at = i % 2
        rows = tok[8 * i:8 * i + 10].reshape(160, C).astype(F32)[8:152]
        for b in range(6):
            act_s[at, b, 0:128, :] = act_of(rows, 128, b)
        pairs[4 * i:4 * i + 4] = paired(at, 64, 0).reshape(4, HALF, C2)


    def project(first, beside, ends=None):
        rows = pairs[first:first + 8].reshape(128, C2)
        if ends is not None:
            rows = jnp.concatenate([rows, ends], axis=0)
        for nb in range(3):
            cols = pl.ds(nb * 512, 512)
            panel = gelu(jnp.dot(rows, down[:, cols], preferred_element_type=F32))
            for n in range(8):
                value = (panel[n * HALF:n * HALF + HALF] * one_if(my_count - (first + n))).astype(BF16)
                panels[first + n, :, cols] = value
                qf[8 + (first + n) * HALF:8 + (first + n + 1) * HALF, cols] = value.astype(F32)
            if ends is not None:
                low_live = one_if(me) * one_if(counts_s[0, dn] - (GROUPS_DEV - 1))
                high_live = one_if(N_SEQ - 1 - me) * one_if(counts_s[0, up])
                beyond = panel[128:136].astype(BF16).astype(F32)
                qf[4:8, cols] = beyond[0:4] * low_live
                qf[520:524, cols] = beyond[4:8] * high_live
            if nb < len(beside):
                four_groups(beside[nb])

    for i in (2, 3, 4, 5):
        four_groups(i)

    for load in loads[2:5]:
        load.wait()

    def set_amount(j, carry):
        slot = slot_s[0, me * GROUPS_DEV + j]
        weight = (1 + 255 * jnp.minimum(slot, 1)) * (1 + 255 * jnp.clip(slot - 1, 0, 1)) * (
            1 + 255 * jnp.clip(slot - 2, 0, 1))
        amount_s[j] = j * weight
        return carry

    lax.fori_loop(0, GROUPS_DEV, set_amount, 0)

    def set_inv(d, carry):
        held = jnp.int32(0)
        for j in range(GROUPS_DEV):
            away = jnp.abs(owner_s[0, me * GROUPS_DEV + j] - d)
            held = held + amount_s[j] * (1 - jnp.minimum(away, 1))
        for slot in range(CAP):
            inv_s[d * CAP + slot] = jnp.minimum((held // 256 ** slot) % 256, GROUPS_DEV - 1)
        return carry

    lax.fori_loop(0, N_SEQ, set_inv, 0)
    my_count = counts_s[0, me]
    loads[5].wait()
    for load in loads[6:]:
        load.start()
    project(8, (0, 1))
    project(16, (6, 7))

    for h in halos:
        h.wait_recv()
    low = jnp.concatenate(
        [halo[0].astype(F32) * one_if(me), tok[1:4].reshape(48, C).astype(F32)], axis=0)
    high = jnp.concatenate(
        [tok[62:65].reshape(48, C).astype(F32), halo[1].astype(F32) * one_if(N_SEQ - 1 - me)], axis=0)
    for b in range(6):
        act_s[0, b, 0:40, :] = act_of(low, 40, b)
        act_s[1, b, 0:40, :] = act_of(high[8:64], 40, b)
    pairs[0] = paired(0, 16, 8)
    pairs[GROUPS_DEV - 1] = paired(1, 16, 0)
    zero = jnp.zeros((8, C2), BF16)
    ends = jnp.concatenate([paired(0, 4, 0), paired(1, 4, 32), zero], axis=0)
    project(0, ())
    project(24, (), ends)

    sends, kept = [], []

    def relay(offsets):
        for kx, kz in offsets:
            dest = seq_at(kx, kz)
            for slot in range(CAP):
                outgoing[dest * CAP + slot] = panels[inv_s[dest * CAP + slot]]
            src = outgoing.at[pl.ds(dest * CAP, CAP)]
            dst = owned_ref.at[0, pl.ds(me * CAP, CAP)]
            if (kx, kz) == (0, 0):
                own = pltpu.make_async_copy(src, dst, own_sem)
                own.start()
                kept.append(own)
            else:
                k = kx * 2 + kz - 1
                send = pltpu.make_async_remote_copy(
                    src, dst, a_send.at[k], a_recv.at[k],
                    device_id=(dp, dest), device_id_type=MESH)
                send.start()
                sends.append(send)

    relay(ORDER[0])

    loads[6].wait()
    loads[7].wait()
    loads[8].wait()

    def mix(r):
        base = r * 128
        for cb in range(6):
            cols = pl.ds(cb * 256, 256)
            v = qf[base:base + 144, cols]
            value = bdw[0:1, cols] * v[7:135] + bdw[1:2, cols] * v[8:136] + bdw[2:3, cols] * v[9:137]
            value = value.astype(BF16)
            mixed[base:base + 128, cols] = value
            mixed_t[pl.ds(cb * 256, 256), base:base + 128] = value.T

    def remote(src, dst, send_sem, recv_sem, device):
        return pltpu.make_async_remote_copy(
            src, dst, send_sem, recv_sem, device_id=device, device_id_type=MESH)

    def copy_core(c):
        return remote(csend.at[c], crecv.at[c], c_send.at[c], c_recv.at[c], (dp_of(my, zh, 1 - core), me))

    def make_term(c):
        cols = pl.ds(c * CW, CW)
        delta = []
        for r in range(4):
            if c == 0:
                mix(r)
            rows = pl.ds(r * 128, 128)
            pre = jnp.dot(mixed[rows, :], bott[:, cols], preferred_element_type=F32)
            value, slope = gelu_both(pre)
            out_ref[0, rows, cols] = value.astype(BF16)
            delta.append((cot[rows, cols].astype(F32) * slope).astype(BF16))
        delta = jnp.concatenate(delta, axis=0)
        for i in range(4):
            part = jnp.dot(mixed_t[pl.ds(i * 384, 384), :], delta, preferred_element_type=F32)
            gbuf[c, pl.ds(i * 4, 4)] = part.reshape(4, 2, 48, CW)
        csend[c] = gbuf[c, :, 1 - core].astype(BF16)
        copy_core(c).start()

    def core_sum(start, width, blocks, count):
        c, lanes = start // CW, pl.ds(start % CW, width)
        rows = pl.ds(blocks, count)
        return gbuf[c, rows, core, :, lanes] + crecv[c, rows, :, lanes].astype(F32)

    class Chunk:
        def __init__(self, n):
            self.start, self.width, self.direct = CHUNKS[n]
            (self.bown, self.ysend, self.yrecv, self.xacc, self.xsend, self.xrecv,
             self.zown, self.zsend, self.zrecv) = chunk_bufs[n]
            self.sems = chunk_sems[n]

        def copy_y(self, n):
            if self.direct:
                src, dst = self.ysend.at[pl.ds(2 * n, 2)], self.yrecv.at[pl.ds(2 * n, 2)]
                to = (my + n + 1) % 4
            else:
                src, dst = self.ysend.at[n], self.yrecv.at[n]
                to = (my + (1 if n < 3 else 3)) % 4
            return remote(src, dst, self.sems[0].at[n], self.sems[1].at[n], (dp_of(to, zh, core), me))

        def copy_x(self, k):
            return remote(self.xsend.at[k - 1], self.xrecv.at[k - 1], self.sems[2].at[k - 1], self.sems[3].at[k - 1],
                          (dp, seq_at(k, 0)))

        def copy_z(self, k):
            to = (dp_of(my, (zh + k // 2) % 4, core), mx * 2 + (mz + k % 2) % 2)
            return remote(self.zsend.at[k], self.zrecv.at[k - 1], self.sems[4].at[k - 1], self.sems[5].at[k - 1], to)

        def begin(self):
            def summed(y, half):
                return core_sum(self.start, self.width, y * 4 + half * 2, 2)

            if self.direct:
                for n in (1, 0, 2):
                    for half in (0, 1):
                        self.ysend[2 * n + half] = summed((my + n + 1) % 4, half).astype(BF16)
                    self.copy_y(n).start()
                self.bown[2] = summed(my, 0)
                self.bown[3] = summed(my, 1)
                return
            nxt, across, prv = (my + 1) % 4, (my + 2) % 4, (my + 3) % 4
            for n, block, half in ((0, across, 0), (3, across, 1), (1, nxt, 1), (4, prv, 0)):
                self.ysend[n] = summed(block, half).astype(BF16)
                self.copy_y(n).start()
            self.bown[0] = summed(nxt, 0)
            self.bown[1] = summed(prv, 1)
            self.bown[2] = summed(my, 0)
            self.bown[3] = summed(my, 1)

        def pass_y(self):
            if self.direct:
                return
            self.copy_y(0).wait_recv()
            self.ysend[2] = (self.bown[0] + self.yrecv[0].astype(F32)).astype(BF16)
            self.copy_y(2).start()
            self.copy_y(3).wait_recv()
            self.ysend[5] = (self.bown[1] + self.yrecv[3].astype(F32)).astype(BF16)
            self.copy_y(5).start()

        def after_y(self):
            if self.direct:
                for n in range(3):
                    self.copy_y(n).wait_recv()
                slots = (0, 2, 4), (1, 3, 5)
            else:
                for n in (1, 4, 2, 5):
                    self.copy_y(n).wait_recv()
                slots = (2, 4), (1, 5)
            half0, half1 = self.bown[2], self.bown[3]
            for n in slots[0]:
                half0 = half0 + self.yrecv[n].astype(F32)
            for n in slots[1]:
                half1 = half1 + self.yrecv[n].astype(F32)
            for h in range(2):
                self.xacc[h] = half0[h].reshape(4, 12, self.width)
                self.xacc[2 + h] = half1[h].reshape(4, 12, self.width)
            for k in (2, 1, 3):
                part = self.xacc[:, (mx + k) % 4]
                self.xsend[k - 1] = part.reshape(48, self.width).astype(BF16)
                self.copy_x(k).start()

        def after_x(self):
            total = self.xacc[:, mx].reshape(48, self.width)
            for k in range(1, 4):
                self.copy_x(k).wait_recv()
                total = total + self.xrecv[k - 1].astype(F32)
            for z in range(8):
                k = ((z // 2 + 4 - zh) % 4) * 2 + (z % 2 + 2 - mz) % 2
                part = pack8(total[z * 6:z * 6 + 6])
                self.zown[k] = part
                self.zsend[k] = part.astype(BF16)
            for k in (4, 5, 3, 7, 2, 6, 1):
                self.copy_z(k).start()

        def after_z(self):
            total = self.zown[0]
            for k in range(1, 8):
                self.copy_z(k).wait_recv()
                total = total + self.zrecv[k - 1].astype(F32)
            grad_ref[:, self.start:self.start + self.width] = unpack8(total, self.width)

        def finish(self):
            for n in range(3 if self.direct else 6):
                self.copy_y(n).wait_send()
            for k in range(1, 4):
                self.copy_x(k).wait_send()
            for k in range(1, 8):
                self.copy_z(k).wait_send()

    chunks = [Chunk(n) for n in range(len(CHUNKS))]
    early, middle, late = ([x for x in chunks if x.start // CW == c] for c in range(NC))

    def each(part, step):
        for x in part:
            getattr(x, step)()

    make_term(0)
    relay(ORDER[1])
    make_term(1)
    copy_core(0).wait_recv()
    each(early, "begin")
    relay(ORDER[2])
    make_term(2)
    copy_core(1).wait_recv()
    each(middle, "begin")
    relay(ORDER[3])
    each(early, "pass_y")
    copy_core(2).wait_recv()
    each(late, "begin")
    relay(ORDER[4])
    each(middle, "pass_y")
    each(early, "after_y")
    each(late, "pass_y")
    each(middle, "after_y")
    each(early, "after_x")
    each(late, "after_y")
    each(middle, "after_x")
    each(late, "after_x")
    each(chunks, "after_z")

    for send in sends:
        send.wait()
    kept[0].wait()
    for h in halos:
        h.wait_send()
    for c in range(NC):
        copy_core(c).wait_send()
    each(chunks, "finish")


CHUNKS = ((0, 256, False), (256, 256, False), (512, 256, False))


def chunk_buffers(width):
    V = pltpu.VMEM
    return (
        V((4, 2, 48, width), F32), V((6, 2, 48, width), BF16), V((6, 2, 48, width), BF16),
        V((4, 4, 12, width), F32), V((3, 48, width), BF16), V((3, 48, width), BF16),
        V((8, 16, 128), F32), V((8, 16, 128), BF16), V((7, 16, 128), BF16),
    )


OUTS = (
    jax.ShapeDtypeStruct((1, GROUPS_DEV, HALF, C2), BF16),
    jax.ShapeDtypeStruct((1, HROWS, C), BF16),
    jax.ShapeDtypeStruct((6, C), F32),
)
FAR = pl.BlockSpec(memory_space=pl.ANY)


def hand_over(owned_ref, out_ref, grad_ref, owned_to, out_to, grad_to, sems):
    copies = [pltpu.make_async_copy(grad_ref, grad_to, sems.at[0])]
    for i in range(4):
        rows = pl.ds(i * 8, 8)
        copies.append(pltpu.make_async_copy(owned_ref.at[0, rows], owned_to.at[0, rows], sems.at[1 + i]))
    for i in range(2):
        rows = pl.ds(i * 256, 256)
        copies.append(pltpu.make_async_copy(out_ref.at[0, rows], out_to.at[0, rows], sems.at[5 + i]))
    for copy in copies:
        copy.start()
    for copy in copies:
        copy.wait()


def on_device(tokens, depthwise_weight, down_weight, bott_dw, bott_weight, cotangent,
              plan_owner, plan_slot, counts):
    V, S, DMA = pltpu.VMEM, pltpu.SMEM, pltpu.SemaphoreType.DMA
    made = pl.pallas_call(
        kernel,
        out_shape=tuple(pltpu.VMEM(o.shape, o.dtype) for o in OUTS),
        in_specs=[FAR] * 9,
        out_specs=(pl.BlockSpec(memory_space=pltpu.VMEM),) * 3,
        scratch_shapes=[
            S((1, 256), jnp.int32),
            S((1, 256), jnp.int32),
            S((1, 8), jnp.int32),
            S((GROUPS_DEV,), jnp.int32),
            S((GROUPS_DEV,), jnp.int32),
            V((3, C), F32),
            V((3, C2), F32),
            V((ROWS // PAD + 2, PAD, C), BF16),
            V((2, PAD, C), BF16),
            V((C2, C2), BF16),
            V((C2, C), BF16),
            V((HROWS, C), BF16),
            V((2, 6, 128, 128), F32),
            V((GROUPS_DEV, HALF, C2), BF16),
            V((GROUPS_DEV, HALF, C2), BF16),
            V((GROUPS_DEV, HALF, C2), BF16),
            V((HROWS + 16, C2), F32),
            V((HROWS, C2), BF16),
            V((C2, HROWS), BF16),
            V((NC, 16, 2, 48, CW), F32),
            V((NC, 16, 48, CW), BF16),
            V((NC, 16, 48, CW), BF16),
            tuple(chunk_buffers(width) for _, width, _ in CHUNKS),
            DMA((9,)), DMA((2,)), DMA((2,)), DMA((7,)), DMA((7,)), DMA,
            DMA((NC,)), DMA((NC,)),
            tuple((DMA((6,)), DMA((6,)), DMA((3,)), DMA((3,)), DMA((7,)), DMA((7,))) for _ in CHUNKS),
        ],
        compiler_params=pltpu.CompilerParams(
            collective_id=0, has_side_effects=True, vmem_limit_bytes=56 * 1024 * 1024),
        cost_estimate=pl.CostEstimate(
            flops=5_000_000_000, bytes_accessed=14_000_000, transcendentals=2_000_000),
    )(plan_owner, plan_slot, counts, tokens.reshape(ROWS // PAD, PAD, C), depthwise_weight, down_weight,
      bott_dw, bott_weight, cotangent)
    return pl.pallas_call(
        hand_over,
        out_shape=OUTS,
        in_specs=[FAR] * 3,
        out_specs=(FAR,) * 3,
        scratch_shapes=[DMA((7,))],
        compiler_params=pltpu.CompilerParams(vmem_limit_bytes=40 * 1024 * 1024),
    )(*made)


def solution(mesh):
    placed = (
        P("dp", "seq", None),
        P(),
        P(),
        P(),
        P(),
        P("dp", "seq", None),
        P("dp", None),
        P("dp", None),
        P("dp", None),
    )
    return jax.shard_map(
        on_device,
        mesh=mesh,
        in_specs=placed,
        out_specs=(P("dp", "seq", None, None), P("dp", "seq", None), P(("dp", "seq"), None)),
        check_vma=False,
    )
```

time: 47.3 us -> 46.8 us (0.989)
  no operation moved by 1% of the time
where the time goes in v3:
time: 46.8 us; the launch traced here: 46.7 us
  Pallas kernels  46.1 us (99%)
  between operations  0.64 us (1%)
    pallas_call x1, Pallas kernels, on_device(): pl.pallas_call(kernel, out_shape=tuple((pltpu.VMEM(o.shape, o.dtype) for...  44.6 us
    pallas_call x1, Pallas kernels, on_device(): pl.pallas_call(hand_over, out_shape=OUTS, in_specs=[FAR] * 3, out_specs=(...  1.46 us

profile of v3, /device:TPU:2, one launch (start us, length us, event | category | flops | bytes accessed | tf_op | source)
XLA Modules:
  0.0 46.7 jit_solution(9111274516446912571)
XLA Ops:
  0.6 44.6 %shard_map.112 = (bf16[1,32,16,1536]{3,2,1,0:T(8,128)(2,1)S(1)}, bf16[1,512,768]{2,1,0:T(8,128)(2,1)S(1)}, f32[6,768]{1,0:T(8,128)S(1)}) custom-call(s32[1,256]{1,0:T(1,128)} %owner_ref.1, s32[1,256]{1,0:T(1,128)} %slot_ref.1, s32[1,8]{1,0:T(1,128)} %counts_ref.1, bf16[64,16,768]{2,1,0:T(8,128)(2,1)} %bitcast.1, f32[3,768]{1,0:T(4,128)} %dw_ref.1, ...), custom_call_target="tpu_custom_call" | custom-call | flops 5000000000 | bytes 14000000 | tf_op jit(solution)/shard_map/pallas_call | solution.py:452
  45.3 1.5 %shard_map.113 = (bf16[1,32,16,1536]{3,2,1,0:T(8,128)(2,1)}, bf16[1,512,768]{2,1,0:T(8,128)(2,1)}, f32[6,768]{1,0:T(8,128)}) custom-call(bf16[1,32,16,1536]{3,2,1,0:T(8,128)(2,1)S(1)} %get-tuple-element.6.owned_ref, bf16[1,512,768]{2,1,0:T(8,128)(2,1)S(1)} %get-tuple-element.7.out_ref, f32[6,768]{1,0:T(8,128)S(1)} %get-tuple-element.8.grad_ref), custom_call_target="tpu_custom_call" | custom-call | tf_op jit(solution)/shard_map/pallas_call | solution.py:491

commit v4 on v3

--- a/solution.py
+++ b/solution.py
@@ -20,19 +20,20 @@
 MESH = pl.DeviceIdType.MESH
 K0 = 0.7978845608028654
 K1 = 0.044715
-ORDER = (((2, 1), (1, 1), (3, 1), (0, 1), (2, 0), (1, 0), (3, 0), (0, 0)), (), (), (), ())
+ORDER = ((2, 1), (1, 1), (3, 1), (0, 1), (2, 0), (1, 0), (3, 0))
 BF16, F32 = jnp.bfloat16, jnp.float32
 
 
 def gelu(x):
-    return 0.5 * x * (1.0 + jnp.tanh(K0 * x * (1.0 + K1 * (x * x))))
+    half = 0.5 * x
+    return half + half * jnp.tanh(x * (K0 + (K0 * K1) * (x * x)))
 
 
 def gelu_both(x):
     square = x * x
-    t = jnp.tanh(K0 * x * (1.0 + K1 * square))
-    half = 0.5 * (1.0 + t)
-    slope = half + 0.5 * x * (1.0 - t * t) * (K0 * (1.0 + 3.0 * K1 * square))
+    t = jnp.tanh(x * (K0 + (K0 * K1) * square))
+    half = 0.5 + 0.5 * t
+    slope = half + 0.5 * x * (1.0 - t * t) * (K0 + (3.0 * K0 * K1) * square)
     return x * half, slope
 
 
@@ -57,9 +58,9 @@
     owner_ref, slot_ref, counts_ref, tokens_ref, dw_ref, down_ref, bdw_ref, bott_ref, cot_ref,
     owned_ref, out_ref, grad_ref,
     owner_s, slot_s, counts_s, amount_s, inv_s, dw, bdw,
-    tok, halo, down, bott, cot, act_s, pairs, panels, outgoing, qf, mixed, mixed_t,
+    tok, halo, down, bott, cot, act_s, pairs, panels, outgoing, arrived, qf, mixed, mixed_t,
     gbuf, csend, crecv, chunk_bufs,
-    in_sem, halo_send, halo_recv, a_send, a_recv, own_sem,
+    in_sem, halo_send, halo_recv, a_send, a_recv,
     c_send, c_recv, chunk_sems,
 ):
     dp = lax.axis_index("dp")
@@ -131,6 +132,10 @@
         pairs[4 * i:4 * i + 4] = paired(at, 64, 0).reshape(4, HALF, C2)
 
 
+    def put_q(nb, at, value):
+        for b in range(4):
+            qf[nb * 4 + b, at:at + value.shape[0], :] = value[:, b * 128:b * 128 + 128]
+
     def project(first, beside, ends=None):
         rows = pairs[first:first + 8].reshape(128, C2)
         if ends is not None:
@@ -141,13 +146,13 @@
             for n in range(8):
                 value = (panel[n * HALF:n * HALF + HALF] * one_if(my_count - (first + n))).astype(BF16)
                 panels[first + n, :, cols] = value
-                qf[8 + (first + n) * HALF:8 + (first + n + 1) * HALF, cols] = value.astype(F32)
+                put_q(nb, 8 + (first + n) * HALF, value.astype(F32))
             if ends is not None:
                 low_live = one_if(me) * one_if(counts_s[0, dn] - (GROUPS_DEV - 1))
                 high_live = one_if(N_SEQ - 1 - me) * one_if(counts_s[0, up])
                 beyond = panel[128:136].astype(BF16).astype(F32)
-                qf[4:8, cols] = beyond[0:4] * low_live
-                qf[520:524, cols] = beyond[4:8] * high_live
+                put_q(nb, 4, beyond[0:4] * low_live)
+                put_q(nb, 520, beyond[4:8] * high_live)
             if nb < len(beside):
                 four_groups(beside[nb])
 
@@ -196,31 +201,36 @@
     pairs[GROUPS_DEV - 1] = paired(1, 16, 0)
     zero = jnp.zeros((8, C2), BF16)
     ends = jnp.concatenate([paired(0, 4, 0), paired(1, 4, 32), zero], axis=0)
+
+    relays = {}
+    for kx, kz in ORDER:
+        dest, k = seq_at(kx, kz), kx * 2 + kz
+        for slot in range(CAP):
+            group = inv_s[dest * CAP + slot]
+            outgoing[dest * CAP + slot] = (pairs[group].astype(F32) * one_if(my_count - group)).astype(BF16)
+        relays[k] = pltpu.make_async_remote_copy(
+            outgoing.at[pl.ds(dest * CAP, CAP)], arrived.at[k - 1], a_send.at[k - 1], a_recv.at[k - 1],
+            device_id=(dp, dest), device_id_type=MESH)
+        relays[k].start()
+
+    def settle(offsets):
+        rows = []
+        for kx, kz in offsets:
+            relays[kx * 2 + kz].wait_recv()
+            rows.append(arrived[kx * 2 + kz - 1].reshape(CAP * HALF, C2))
+        rows = jnp.concatenate(rows, axis=0)
+        for nb in range(3):
+            cols = pl.ds(nb * 512, 512)
+            panel = gelu(jnp.dot(rows, down[:, cols], preferred_element_type=F32)).astype(BF16)
+            for n, (kx, kz) in enumerate(offsets):
+                source = ((mx + 4 - kx) % 4) * 2 + (mz + 2 - kz) % 2
+                owned_ref[0, pl.ds(source * CAP, CAP), :, cols] = panel[n * 64:n * 64 + 64].reshape(CAP, HALF, 512)
+
     project(0, ())
     project(24, (), ends)
 
-    sends, kept = [], []
-
-    def relay(offsets):
-        for kx, kz in offsets:
-            dest = seq_at(kx, kz)
-            for slot in range(CAP):
-                outgoing[dest * CAP + slot] = panels[inv_s[dest * CAP + slot]]
-            src = outgoing.at[pl.ds(dest * CAP, CAP)]
-            dst = owned_ref.at[0, pl.ds(me * CAP, CAP)]
-            if (kx, kz) == (0, 0):
-                own = pltpu.make_async_copy(src, dst, own_sem)
-                own.start()
-                kept.append(own)
-            else:
-                k = kx * 2 + kz - 1
-                send = pltpu.make_async_remote_copy(
-                    src, dst, a_send.at[k], a_recv.at[k],
-                    device_id=(dp, dest), device_id_type=MESH)
-                send.start()
-                sends.append(send)
-
-    relay(ORDER[0])
+    for slot in range(CAP):
+        owned_ref[0, me * CAP + slot] = panels[inv_s[me * CAP + slot]]
 
     loads[6].wait()
     loads[7].wait()
@@ -230,8 +240,10 @@
         base = r * 128
         for cb in range(6):
             cols = pl.ds(cb * 256, 256)
-            v = qf[base:base + 144, cols]
-            value = bdw[0:1, cols] * v[7:135] + bdw[1:2, cols] * v[8:136] + bdw[2:3, cols] * v[9:137]
+            value = jnp.concatenate([
+                sum(bdw[tap:tap + 1, b * 128:b * 128 + 128] * qf[b, base + 7 + tap:base + 135 + tap, :]
+                    for tap in range(3))
+                for b in (2 * cb, 2 * cb + 1)], axis=1)
             value = value.astype(BF16)
             mixed[base:base + 128, cols] = value
             mixed_t[pl.ds(cb * 256, 256), base:base + 128] = value.T
@@ -379,32 +391,30 @@
             getattr(x, step)()
 
     make_term(0)
-    relay(ORDER[1])
     make_term(1)
     copy_core(0).wait_recv()
     each(early, "begin")
-    relay(ORDER[2])
     make_term(2)
     copy_core(1).wait_recv()
     each(middle, "begin")
-    relay(ORDER[3])
     each(early, "pass_y")
     copy_core(2).wait_recv()
     each(late, "begin")
-    relay(ORDER[4])
     each(middle, "pass_y")
     each(early, "after_y")
     each(late, "pass_y")
     each(middle, "after_y")
     each(early, "after_x")
     each(late, "after_y")
+    settle(ORDER[0:2])
     each(middle, "after_x")
+    settle(ORDER[2:4])
     each(late, "after_x")
+    settle(ORDER[4:7])
     each(chunks, "after_z")
 
-    for send in sends:
-        send.wait()
-    kept[0].wait()
+    for k in range(1, 8):
+        relays[k].wait_send()
     for h in halos:
         h.wait_send()
     for c in range(NC):
@@ -471,14 +481,15 @@
             V((GROUPS_DEV, HALF, C2), BF16),
             V((GROUPS_DEV, HALF, C2), BF16),
             V((GROUPS_DEV, HALF, C2), BF16),
-            V((HROWS + 16, C2), F32),
+            V((7, CAP, HALF, C2), BF16),
+            V((12, HROWS + 16, 128), F32),
             V((HROWS, C2), BF16),
             V((C2, HROWS), BF16),
             V((NC, 16, 2, 48, CW), F32),
             V((NC, 16, 48, CW), BF16),
             V((NC, 16, 48, CW), BF16),
             tuple(chunk_buffers(width) for _, width, _ in CHUNKS),
-            DMA((9,)), DMA((2,)), DMA((2,)), DMA((7,)), DMA((7,)), DMA,
+            DMA((9,)), DMA((2,)), DMA((2,)), DMA((7,)), DMA((7,)),
             DMA((NC,)), DMA((NC,)),
             tuple((DMA((6,)), DMA((6,)), DMA((3,)), DMA((3,)), DMA((7,)), DMA((7,))) for _ in CHUNKS),
         ],

time: 46.8 us -> 45.3 us (0.968)
  Pallas kernels: 46.1 us -> 44.5 us
    pallas_call x1, Pallas kernels: 44.6 us -> 43.1 us  [on_device(): pl.pallas_call(kernel, out_shape=tuple((pltpu.VMEM(o.shape, o.dtype) for...]
where the time goes in v4:
time: 45.3 us; the launch traced here: 45.2 us
  Pallas kernels  44.5 us (98%)
  between operations  0.64 us (1%)
    pallas_call x1, Pallas kernels, on_device(): pl.pallas_call(kernel, out_shape=tuple((pltpu.VMEM(o.shape, o.dtype) for...  43.1 us
    pallas_call x1, Pallas kernels, on_device(): pl.pallas_call(hand_over, out_shape=OUTS, in_specs=[FAR] * 3, out_specs=(...  1.46 us

profile of v4, /device:TPU:2, one launch (start us, length us, event | category | flops | bytes accessed | tf_op | source)
XLA Modules:
  0.0 45.2 jit_solution(15981529124359244260)
XLA Ops:
  0.6 43.1 %shard_map.112 = (bf16[1,32,16,1536]{3,2,1,0:T(8,128)(2,1)S(1)}, bf16[1,512,768]{2,1,0:T(8,128)(2,1)S(1)}, f32[6,768]{1,0:T(8,128)S(1)}) custom-call(s32[1,256]{1,0:T(1,128)} %owner_ref.1, s32[1,256]{1,0:T(1,128)} %slot_ref.1, s32[1,8]{1,0:T(1,128)} %counts_ref.1, bf16[64,16,768]{2,1,0:T(8,128)(2,1)} %bitcast.1, f32[3,768]{1,0:T(4,128)} %dw_ref.1, ...), custom_call_target="tpu_custom_call" | custom-call | flops 5000000000 | bytes 14000000 | tf_op jit(solution)/shard_map/pallas_call | solution.py:462
  43.7 1.5 %shard_map.113 = (bf16[1,32,16,1536]{3,2,1,0:T(8,128)(2,1)}, bf16[1,512,768]{2,1,0:T(8,128)(2,1)}, f32[6,768]{1,0:T(8,128)}) custom-call(bf16[1,32,16,1536]{3,2,1,0:T(8,128)(2,1)S(1)} %get-tuple-element.6.owned_ref, bf16[1,512,768]{2,1,0:T(8,128)(2,1)S(1)} %get-tuple-element.7.out_ref, f32[6,768]{1,0:T(8,128)S(1)} %get-tuple-element.8.grad_ref), custom_call_target="tpu_custom_call" | custom-call | tf_op jit(solution)/shard_map/pallas_call | solution.py:502

commit v5 on v4

--- a/solution.py
+++ b/solution.py
@@ -422,7 +422,7 @@
     each(chunks, "finish")
 
 
-CHUNKS = ((0, 256, False), (256, 256, False), (512, 256, False))
+CHUNKS = ((0, 256, False), (256, 256, False), (512, 256, True))
 
 
 def chunk_buffers(width):

time: 45.3 us -> 45 us (level)
  Pallas kernels: 44.5 us -> 44 us
    pallas_call x1, Pallas kernels: 43.1 us -> 42.6 us  [on_device(): pl.pallas_call(kernel, out_shape=tuple((pltpu.VMEM(o.shape, o.dtype) for...]
where the time goes in v5:
time: 45 us; the launch traced here: 44.7 us
  Pallas kernels  44 us (98%)
  between operations  0.64 us (1%)
    pallas_call x1, Pallas kernels, on_device(): pl.pallas_call(kernel, out_shape=tuple((pltpu.VMEM(o.shape, o.dtype) for...  42.6 us
    pallas_call x1, Pallas kernels, on_device(): pl.pallas_call(hand_over, out_shape=OUTS, in_specs=[FAR] * 3, out_specs=(...  1.46 us

profile of v5, /device:TPU:2, one launch (start us, length us, event | category | flops | bytes accessed | tf_op | source)
XLA Modules:
  0.0 44.7 jit_solution(11100343628469663303)
XLA Ops:
  0.6 42.6 %shard_map.112 = (bf16[1,32,16,1536]{3,2,1,0:T(8,128)(2,1)S(1)}, bf16[1,512,768]{2,1,0:T(8,128)(2,1)S(1)}, f32[6,768]{1,0:T(8,128)S(1)}) custom-call(s32[1,256]{1,0:T(1,128)} %owner_ref.1, s32[1,256]{1,0:T(1,128)} %slot_ref.1, s32[1,8]{1,0:T(1,128)} %counts_ref.1, bf16[64,16,768]{2,1,0:T(8,128)(2,1)} %bitcast.1, f32[3,768]{1,0:T(4,128)} %dw_ref.1, ...), custom_call_target="tpu_custom_call" | custom-call | flops 5000000000 | bytes 14000000 | tf_op jit(solution)/shard_map/pallas_call | solution.py:462
  43.2 1.5 %shard_map.113 = (bf16[1,32,16,1536]{3,2,1,0:T(8,128)(2,1)}, bf16[1,512,768]{2,1,0:T(8,128)(2,1)}, f32[6,768]{1,0:T(8,128)}) custom-call(bf16[1,32,16,1536]{3,2,1,0:T(8,128)(2,1)S(1)} %get-tuple-element.6.owned_ref, bf16[1,512,768]{2,1,0:T(8,128)(2,1)S(1)} %get-tuple-element.7.out_ref, f32[6,768]{1,0:T(8,128)S(1)} %get-tuple-element.8.grad_ref), custom_call_target="tpu_custom_call" | custom-call | tf_op jit(solution)/shard_map/pallas_call | solution.py:502
